TPU v7x, 32 devices: a whole 2x2x4 slice. The times are simulated.
32 devices in a mesh: dp: 4 (over y, core), seq: 8 (over z, x).
Axes of the slice: x: 2, y: 2, z: 4, core: 2. Of those that a mesh axis runs over, the one named last changes fastest.
Arguments:
- x_in: bfloat16 [4, 2048, 2048], P('dp', 'seq'), may hold values from -0.37 to 0.37
- b_in: bfloat16 [4, 2048, 128], P('dp', 'seq'), may hold values from -7.4 to 7.4
- c_in: bfloat16 [4, 2048, 128], P('dp', 'seq'), may hold values from -0.12988281 to 0.12988281
- dt: float32 [4, 32, 2048], P('dp', None, 'seq'), may hold values from 0.2 to 8192, as said below
- a_log: float32 [32], replicated, may hold values from -14 to -2, as said below
- skip: float32 [32], replicated, may hold values from 1 to 3
- cotangent: bfloat16 [4, 2048, 2048], P('dp', 'seq'), may hold values from -0.29882812 to 0.29882812
Outputs:
- y_out: bfloat16 [4, 2048, 2048], P('dp', 'seq')
- grad_x: bfloat16 [4, 2048, 2048], P('dp', 'seq')
- grad_b: bfloat16 [4, 2048, 128], P('dp', 'seq')
- grad_c: bfloat16 [4, 2048, 128], P('dp', 'seq')
- grad_dt: float32 [4, 32, 2048], P('dp', None, 'seq')
- grad_alog: float32 [32], replicated
- derivative_bypass: float32 [32], replicated
Inputs may be any that keep to these rules, and one draw needn't show every extreme that they name: `dt`: positive step sizes. Each head's decay rate exp(a_log) is positive.
All inputs are finite; a program needn't handle non-finite values.
Results may differ from a plain program's by a relative error of at most 0.018.
Values sent between devices are 32-bit elements; how exact they have to be, the bound alone decides.
A program may use at most 128 MiB of HBM per device.

v0:
```python
import functools

import jax
import jax.numpy as jnp
from jax import lax
from jax.experimental import pallas as pl
from jax.experimental.pallas import tpu as pltpu
from jax.sharding import PartitionSpec as P

F32 = jnp.float32
BF16 = jnp.bfloat16
MESH = pl.DeviceIdType.MESH
LANES = 128
VMEM_BYTES = 62 * 1024 * 1024


def dot(a, b, ca=1, cb=0, precision=None):
    return lax.dot_general(
        a, b, (((ca,), (cb,)), ((), ())), preferred_element_type=F32, precision=precision
    )


def pack(v, heads):
    lane = lax.broadcasted_iota(jnp.int32, v.shape, 1)
    hi = v.astype(BF16).astype(F32)
    rest = v - hi
    mid = rest.astype(BF16).astype(F32)
    low = rest - mid
    out = jnp.where(lane < heads, hi, jnp.where(lane < 2 * heads, mid, low))
    return jnp.where(lane < 3 * heads, out, 0.0).astype(BF16)


def halves(v):
    hi = v.astype(BF16)
    return hi, (v - hi.astype(F32)).astype(BF16)


def kernel(
    n_seq,
    n_dp,
    width,
    x_hbm,
    b_hbm,
    c_hbm,
    dt_hbm,
    alog_hbm,
    skip_hbm,
    g_hbm,
    y_hbm,
    gx_hbm,
    gb_hbm,
    gc_hbm,
    gdt_hbm,
    ga_ref,
    gs_ref,
    y_ref,
    gx_ref,
    gb_ref,
    gc_ref,
    gdt_ref,
    x_ref,
    b_ref,
    c_ref,
    dt_ref,
    alog_ref,
    skip_ref,
    g_ref,
    spread,
    cum_rows,
    cum_pack,
    e_wide,
    to_wide,
    scaled,
    dv,
    bt,
    ct,
    local,
    p_in,
    p_out,
    other_local,
    entry,
    m_out,
    rows,
    y_acc,
    dx_acc,
    cb_ref,
    dcb,
    dc_acc,
    db_acc,
    dcum,
    gain_own,
    gain_in,
    red_seq,
    red_dp,
    p_send,
    p_recv,
    m_send,
    m_recv,
    l_send,
    l_recv,
    g_sem,
    load_sem,
    store_sem,
    rs_send,
    rs_recv,
    rd_send,
    rd_recv,
):
    heads, span = dt_ref.shape
    feat = x_ref.shape[1]
    size = feat // heads
    chunks = feat // width
    pairs = n_seq // 2
    me = lax.axis_index("seq")
    mine = lax.axis_index("dp")
    place = me // 2
    odd = lax.rem(me, 2)
    partner = me + 1 - 2 * odd

    moves = [
        pltpu.make_async_copy(src, dst, load_sem.at[i])
        for i, (src, dst) in enumerate(
            [
                (dt_hbm, dt_ref),
                (alog_hbm, alog_ref),
                (skip_hbm, skip_ref),
                (b_hbm, b_ref),
                (c_hbm, c_ref),
                (x_hbm, x_ref),
                (g_hbm, g_ref),
            ]
        )
    ]
    for move in moves:
        move.start()
    barrier = pltpu.get_barrier_semaphore()

    def greet_seq(o, carry):
        pl.semaphore_signal(
            barrier, inc=1, device_id={"seq": lax.rem(me + o, n_seq)}, device_id_type=MESH
        )
        return carry

    def greet_dp(o, carry):
        pl.semaphore_signal(
            barrier, inc=1, device_id={"dp": lax.rem(mine + o, n_dp)}, device_id_type=MESH
        )
        return carry

    lax.fori_loop(1, n_seq, greet_seq, 0)
    lax.fori_loop(1, n_dp, greet_dp, 0)

    diag = lax.broadcasted_iota(jnp.int32, (heads, heads), 0) == lax.broadcasted_iota(
        jnp.int32, (heads, heads), 1
    )

    def column(row):
        return jnp.sum(jnp.where(diag, jnp.broadcast_to(row, (heads, heads)), 0.0), 1, keepdims=True)

    def as_row(col):
        return jnp.sum(jnp.where(diag, jnp.broadcast_to(col, (heads, heads)), 0.0), 0, keepdims=True)

    for move in moves[:3]:
        move.wait()
    rate = jnp.exp(column(alog_ref[...]))
    la = -rate * dt_ref[...]
    t_row = lax.broadcasted_iota(jnp.int32, (span, span), 0)
    t_col = lax.broadcasted_iota(jnp.int32, (span, span), 1)
    upper = jnp.where(t_row <= t_col, 1.0, 0.0).astype(F32)
    cum = dot(jnp.concatenate([la] * (LANES // heads), 0), upper, precision=lax.Precision.HIGHEST)
    cum_rows[...] = cum
    cum_t = jnp.transpose(cum)
    cum_pack[...] = pack(cum_t, heads)
    e_t = jnp.exp(cum_t)
    gain_own[...] = e_t[span - 16 :, :]
    pl.semaphore_wait(barrier, n_seq - 1 + n_dp - 1)
    gain_copy = pltpu.make_async_remote_copy(
        src_ref=gain_own,
        dst_ref=gain_in,
        send_sem=g_sem.at[0],
        recv_sem=g_sem.at[1],
        device_id={"seq": partner},
        device_id_type=MESH,
    )
    gain_copy.start()

    e_pack = pack(e_t, heads)
    to_pack = pack(jnp.exp(cum_t[span - 1 :, :] - cum_t), heads)
    spread_row = lax.rem(lax.broadcasted_iota(jnp.int32, spread.shape, 0), heads)
    spread_col = lax.broadcasted_iota(jnp.int32, spread.shape, 1) // size
    spread[...] = jnp.where(spread_row == spread_col, 1.0, 0.0).astype(BF16)
    for move in moves[3:]:
        move.wait()
    bt[...] = jnp.transpose(b_ref[...].astype(F32)).astype(BF16)
    ct[...] = jnp.transpose(c_ref[...].astype(F32)).astype(BF16)
    skip_col = jnp.broadcast_to(column(skip_ref[...]), (heads, LANES))
    skip_pack = pack(jnp.transpose(jnp.concatenate([skip_col] * (LANES // heads), 0)), heads)

    def part(c):
        return pl.ds(pl.multiple_of(c * width, width), width)

    cb_ref[...] = dot(c_ref[...], b_ref[...], 1, 1)
    dcb[...] = jnp.zeros_like(dcb)

    def role(d):
        lead = odd == d
        steps = jnp.where(d == 0, place, pairs - 1 - place)
        lead_row = jnp.broadcast_to(jnp.where(lead, 1, 0), (1, width)) == 1
        return lead, steps, lead_row

    def p_copy(d, c):
        return pltpu.make_async_remote_copy(
            src_ref=p_out.at[d, c],
            dst_ref=p_in.at[d, c],
            send_sem=p_send.at[d, c],
            recv_sem=p_recv.at[d, c],
            device_id={"seq": lax.rem(me + 2 - 4 * d + n_seq, n_seq)},
            device_id_type=MESH,
        )

    def m_copy(d, c):
        return pltpu.make_async_remote_copy(
            src_ref=m_out.at[d, c],
            dst_ref=entry.at[d, c],
            send_sem=m_send.at[d, c],
            recv_sem=m_recv.at[d, c],
            device_id={"seq": partner},
            device_id_type=MESH,
        )

    def l_copy(d, c):
        return pltpu.make_async_remote_copy(
            src_ref=local.at[d, c],
            dst_ref=other_local.at[d, c],
            send_sem=l_send.at[d, c],
            recv_sem=l_recv.at[d, c],
            device_id={"seq": partner},
            device_id_type=MESH,
        )

    half = chunks // 2
    blank = jnp.zeros((LANES, width), F32)

    def step(d, c):
        lead, steps, lead_row = role(d)
        cols = part(c)
        own = rows[0:1, cols]
        other = rows[1:2, cols]
        wanted = jnp.logical_or(jnp.logical_not(lead), steps < pairs - 1)

        @pl.when(wanted)
        def _():
            l_copy(d, c).wait_recv()

        @pl.when(jnp.logical_not(wanted))
        def _():
            other_local[d, c] = blank

        @pl.when(steps > 0)
        def _():
            p_copy(d, c).wait_recv()

        @pl.when(steps == 0)
        def _():
            p_in[d, c] = blank

        before = p_in[d, c]
        here = local[d, c]
        there = other_local[d, c]

        @pl.when(steps < pairs - 1)
        def _():
            p_out[d, c] = own * other * before + jnp.where(
                lead_row, other * here + there, own * there + here
            )
            p_copy(d, c).start()

        m_out[d, c] = jnp.where(lead_row, own * before + here, before)

        @pl.when(jnp.logical_or(lead, steps > 0))
        def _():
            m_copy(d, c).start()

        entry[d, c] = jnp.where(lead_row, before, other * before + there)

    def prepare(i, carry):
        c = lax.rem(i + (1 - odd) * half, chunks)
        cols = part(c)
        spread_c = spread[:, cols]
        e_c = dot(e_pack, spread_c)
        to_c = dot(to_pack, spread_c)
        e_wide[:, cols] = e_c
        to_wide[:, cols] = to_c
        x_c = x_ref[:, cols].astype(F32)
        g_c = g_ref[:, cols].astype(F32)
        sc = (x_c * to_c).astype(BF16)
        dv_c = (g_c * e_c).astype(BF16)
        scaled[:, cols] = sc
        dv[:, cols] = dv_c
        local[0, c] = dot(bt[...], sc)
        local[1, c] = dot(ct[...], dv_c)
        rows[0:1, cols] = e_c[span - 1 :, :]
        rows[2:3, cols] = dot(skip_pack[0:16], spread_c)[0:1]
        rows[4:5, cols] = jnp.sum(x_c * g_c, 0, keepdims=True)

        for d in range(2):
            lead, steps, _ = role(d)
            wanted = jnp.logical_or(lead, steps < pairs - 1)

            @pl.when(jnp.logical_and(i < half, wanted))
            def _():
                l_copy(d, c).start()

        return carry

    lax.fori_loop(0, chunks, prepare, 0)
    gain_copy.wait()
    gain_pack = pack(gain_in[...], heads)
    rows[1:2, :] = dot(gain_pack, spread[...])[15:16, :]


    def inner(j, carry):
        cols = pl.ds(pl.multiple_of(j * 2 * size, 2 * size), 2 * size)
        x2 = x_ref[:, cols]
        g2 = g_ref[:, cols]
        lane = lax.broadcasted_iota(jnp.int32, (span, 2 * size), 1)
        lower = t_row >= t_col
        y2, dx2 = [], []
        total = dcb[...]
        for i in range(2):
            h = 2 * j + i
            pick_row = lax.broadcasted_iota(jnp.int32, (LANES, span), 0)
            pick = jnp.where(lax.rem(pick_row, heads) == h, 1.0, 0.0).astype(BF16)
            at_t = dot(cum_pack[...], pick)
            decay = jnp.exp(jnp.where(lower, at_t - cum_rows[pl.ds(h, 1), :], -1e30))
            weights = (cb_ref[...] * decay).astype(BF16)
            y2.append(dot(weights, x2))
            dx2.append(dot(weights, g2, 0, 0))
            own_lanes = (lane < size) if i == 0 else (lane >= size)
            g_own = jnp.where(own_lanes, g2.astype(F32), 0.0).astype(BF16)
            total = total + dot(g_own, x2, 1, 1) * decay
        dcb[...] = total
        y_acc[:, cols] = jnp.where(lane < size, y2[0], y2[1])
        dx_acc[:, cols] = jnp.where(lane < size, dx2[0], dx2[1])
        return carry

    per_chunk = width // (2 * size)
    upper_half = jnp.where(place >= pairs // 2, 1, 0)

    def middle(i, carry):
        late = i // half
        step(upper_half + late - 2 * late * upper_half, lax.rem(i, half) + odd * half)
        return lax.fori_loop(i * per_chunk, (i + 1) * per_chunk, inner, carry)

    lax.fori_loop(0, chunks, middle, 0)

    dcb_low = dcb[...]
    dc_acc[...] = dot(dcb_low.astype(BF16), b_ref[...])
    db_acc[...] = dot(jnp.transpose(dcb_low).astype(BF16), c_ref[...])
    dcum[...] = jnp.zeros_like(dcum)

    def finish(i, carry):
        c = lax.rem(i + odd * half, chunks)
        cols = part(c)
        for d in range(2):
            lead, steps, _ = role(d)
            nothing = jnp.logical_and(lead, steps == 0)

            @pl.when(jnp.logical_and(i >= half, nothing))
            def _():
                entry[d, c] = blank

            @pl.when(jnp.logical_and(i >= half, jnp.logical_not(nothing)))
            def _():
                m_copy(d, c).wait_recv()

        state = entry[0, c]
        adj = entry[1, c]
        state_low = state.astype(BF16)
        adj_low = adj.astype(BF16)
        x_c = x_ref[:, cols].astype(F32)
        g_c = g_ref[:, cols].astype(F32)
        skip_c = rows[2:3, cols]
        y_c = y_acc[:, cols] + e_wide[:, cols] * dot(c_ref[...], state_low)
        y_ref[:, cols] = (y_c + skip_c * x_c).astype(BF16)
        dx_state = to_wide[:, cols] * dot(b_ref[...], adj_low)
        dx_c = dx_acc[:, cols] + dx_state
        gx_ref[:, cols] = (dx_c + skip_c * g_c).astype(BF16)
        dc_acc[...] += dot(dv[:, cols], state_low, 1, 1)
        db_acc[...] += dot(scaled[:, cols], adj_low, 1, 1)
        hi, low = halves(g_c * y_c - x_c * dx_c)
        sel = spread[0:heads, cols]
        dcum[...] += dot(sel, hi, 1, 1) + dot(sel, low, 1, 1)
        rows[3:4, cols] = jnp.sum(x_c * dx_state, 0, keepdims=True) + rows[0:1, cols] * jnp.sum(
            state * adj, 0, keepdims=True
        )
        return carry

    lax.fori_loop(0, chunks, finish, 0)

    gc_ref[...] = dc_acc[...].astype(BF16)
    gb_ref[...] = db_acc[...].astype(BF16)
    sums = jnp.concatenate([rows[3:5, :], jnp.zeros((14, feat), F32)], 0)
    hi, low = halves(sums)
    sel = spread[0:heads, :]
    per_head = dot(sel, hi, 1, 1) + dot(sel, low, 1, 1)
    lower_f = jnp.where(t_row >= t_col, 1.0, 0.0).astype(F32)
    dla = dot(dcum[...], lower_f, precision=lax.Precision.HIGHEST) + per_head[:, 0:1]
    gdt_ref[...] = -rate * dla
    alog_row = as_row(jnp.sum(dla * la, 1, keepdims=True))
    skip_row = as_row(per_head[:, 1:2])

    stores = [
        pltpu.make_async_copy(src, dst, store_sem.at[i])
        for i, (src, dst) in enumerate(
            [
                (y_ref, y_hbm),
                (gx_ref, gx_hbm),
                (gb_ref, gb_hbm),
                (gc_ref, gc_hbm),
                (gdt_ref, gdt_hbm),
            ]
        )
    ]
    for move in stores:
        move.start()
    red_seq[me] = jnp.zeros((8, LANES), F32)
    red_seq[me, 0:1, 0:heads] = alog_row
    red_seq[me, 1:2, 0:heads] = skip_row

    def share(axis, here, count, buf, send, recv):
        def copy(target, slot, o):
            return pltpu.make_async_remote_copy(
                src_ref=buf.at[here],
                dst_ref=buf.at[slot],
                send_sem=send.at[o],
                recv_sem=recv.at[slot],
                device_id={axis: target},
                device_id_type=MESH,
            )

        def go(o, carry):
            copy(lax.rem(here + o, count), here, o).start()
            return carry

        def come(o, carry):
            source = lax.rem(here + o, count)
            copy(source, source, o).wait_recv()
            copy(source, here, o).wait_send()
            return carry

        lax.fori_loop(1, count, go, 0)
        lax.fori_loop(1, count, come, 0)
        return jnp.sum(buf[...], 0)

    red_dp[mine] = share("seq", me, n_seq, red_seq, rs_send, rs_recv)
    total = share("dp", mine, n_dp, red_dp, rd_send, rd_recv)
    ga_ref[...] = total[0:1, 0:heads]
    gs_ref[...] = total[1:2, 0:heads]

    def drain(i, carry):
        c = i + odd * half
        away = i + (1 - odd) * half
        for d in range(2):
            lead, steps, _ = role(d)

            @pl.when(steps < pairs - 1)
            def _():
                p_copy(d, c).wait_send()

            @pl.when(jnp.logical_or(lead, steps > 0))
            def _():
                m_copy(d, c).wait_send()

            @pl.when(jnp.logical_or(lead, steps < pairs - 1))
            def _():
                l_copy(d, away).wait_send()

        return carry

    lax.fori_loop(0, half, drain, 0)
    for move in stores:
        move.wait()


def write_out(count, *refs):
    held = refs[2 * count : 3 * count]
    load, store = refs[3 * count :]
    loads = [pltpu.make_async_copy(refs[i], held[i], load.at[i]) for i in range(count)]
    stores = [
        pltpu.make_async_copy(held[i], refs[count + i], store.at[i]) for i in range(count)
    ]
    for copy in loads:
        copy.start()
    for first, second in zip(loads, stores):
        first.wait()
        second.start()
    for copy in stores:
        copy.wait()


def shards(n_seq, n_dp, x_in, b_in, c_in, dt, a_log, skip, cotangent):
    _, span, feat = x_in.shape
    state_dim = b_in.shape[2]
    heads = a_log.shape[0]
    width = 256
    chunks = feat // width
    blocks = (2, chunks, state_dim, width)
    vmem = pl.BlockSpec(memory_space=pltpu.VMEM)
    hbm = pl.BlockSpec(memory_space=pltpu.HBM)
    dma = pltpu.SemaphoreType.DMA
    wide = pltpu.VMEM((span, feat), F32)
    wide_low = pltpu.VMEM((span, feat), BF16)
    outs = pl.pallas_call(
        functools.partial(kernel, n_seq, n_dp, width),
        out_shape=(
            jax.ShapeDtypeStruct((span, feat), BF16),
            jax.ShapeDtypeStruct((span, feat), BF16),
            jax.ShapeDtypeStruct((span, state_dim), BF16),
            jax.ShapeDtypeStruct((span, state_dim), BF16),
            jax.ShapeDtypeStruct((heads, span), F32),
            jax.ShapeDtypeStruct((1, heads), F32),
            jax.ShapeDtypeStruct((1, heads), F32),
        ),
        in_specs=[hbm] * 7,
        out_specs=(hbm,) * 5 + (vmem,) * 2,
        scratch_shapes=[
            wide_low,
            wide_low,
            pltpu.VMEM((span, state_dim), BF16),
            pltpu.VMEM((span, state_dim), BF16),
            pltpu.VMEM((heads, span), F32),
            wide_low,
            pltpu.VMEM((span, state_dim), BF16),
            pltpu.VMEM((span, state_dim), BF16),
            pltpu.VMEM((heads, span), F32),
            pltpu.VMEM((1, heads), F32),
            pltpu.VMEM((1, heads), F32),
            wide_low,
            pltpu.VMEM((LANES, feat), BF16),
            pltpu.VMEM((LANES, span), F32),
            pltpu.VMEM((span, LANES), BF16),
            wide,
            wide,
            wide_low,
            wide_low,
            pltpu.VMEM((state_dim, span), BF16),
            pltpu.VMEM((state_dim, span), BF16),
            pltpu.VMEM(blocks, F32),
            pltpu.VMEM(blocks, F32),
            pltpu.VMEM(blocks, F32),
            pltpu.VMEM(blocks, F32),
            pltpu.VMEM(blocks, F32),
            pltpu.VMEM(blocks, F32),
            pltpu.VMEM((8, feat), F32),
            wide,
            wide,
            pltpu.VMEM((span, span), F32),
            pltpu.VMEM((span, span), F32),
            pltpu.VMEM((span, state_dim), F32),
            pltpu.VMEM((span, state_dim), F32),
            pltpu.VMEM((heads, span), F32),
            pltpu.VMEM((16, LANES), F32),
            pltpu.VMEM((16, LANES), F32),
            pltpu.VMEM((n_seq, 8, LANES), F32),
            pltpu.VMEM((n_dp, 8, LANES), F32),
            dma((2, chunks)),
            dma((2, chunks)),
            dma((2, chunks)),
            dma((2, chunks)),
            dma((2, chunks)),
            dma((2, chunks)),
            dma((2,)),
            dma((7,)),
            dma((5,)),
            dma((n_seq,)),
            dma((n_seq,)),
            dma((n_dp,)),
            dma((n_dp,)),
        ],
        compiler_params=pltpu.CompilerParams(
            collective_id=0, has_side_effects=True, vmem_limit_bytes=VMEM_BYTES
        ),
    )(x_in[0], b_in[0], c_in[0], dt[0], a_log[None], skip[None], cotangent[0])
    y, gx, gb, gc, gdt, ga, gs = pl.pallas_call(
        functools.partial(write_out, len(outs)),
        out_shape=tuple(jax.ShapeDtypeStruct(o.shape, o.dtype) for o in outs),
        in_specs=[hbm] * len(outs),
        out_specs=(hbm,) * len(outs),
        scratch_shapes=[pltpu.VMEM(o.shape, o.dtype) for o in outs]
        + [dma((len(outs),)), dma((len(outs),))],
        compiler_params=pltpu.CompilerParams(vmem_limit_bytes=VMEM_BYTES),
    )(*outs)
    return (y[None], gx[None], gb[None], gc[None], gdt[None], ga[0], gs[0])


def solution(mesh):
    tokens = P("dp", "seq", None)
    steps = P("dp", None, "seq")
    return jax.shard_map(
        functools.partial(shards, mesh.shape["seq"], mesh.shape["dp"]),
        mesh=mesh,
        in_specs=(tokens, tokens, tokens, steps, P(), P(), tokens),
        out_specs=(tokens, tokens, tokens, tokens, steps, P(), P()),
        check_vma=False,
    )
```

profile of v0, /device:TPU:0, one launch (start us, length us, event | category | flops | bytes accessed | tf_op | source)
XLA Modules:
  0.0 65.7 jit_solution(17328105589975696814)
XLA Ops:
  0.6 62.4 %shard_map.126 = (bf16[256,2048]{1,0:T(8,128)(2,1)}, bf16[256,2048]{1,0:T(8,128)(2,1)}, bf16[256,128]{1,0:T(8,128)(2,1)}, bf16[256,128]{1,0:T(8,128)(2,1)}, f32[...) custom-call(bf16[256,2048]{1,0:T(8,128)(2,1)} %bitcast.14, bf16[256,128]{1,0:T(8,128)(2,1)} %bitcast.16, ...), custom_call_target="tpu_custom_call" | custom-call | tf_op jit(solution)/shard_map/pallas_call | solution.py:514
  63.0 2.7 %shard_map.127 = (bf16[256,2048]{1,0:T(8,128)(2,1)}, bf16[256,2048]{1,0:T(8,128)(2,1)}, bf16[256,128]{1,0:T(8,128)(2,1)}, bf16[256,128]{1,0:T(8,128)(2,1)}, f32[...) custom-call(bf16[256,2048]{1,0:T(8,128)(2,1)} %get-tuple-element.21.refs_0_, ...), custom_call_target="tpu_custom_call" | custom-call | tf_op jit(solution)/shard_map/pallas_call | solution.py:585
where the time goes:
time: 65.9 us; the launch traced here: 65.7 us
  Pallas kernels  65.1 us (99%)
    pallas_call x1, Pallas kernels, shards(): pl.pallas_call(functools.partial(kernel, n_seq, n_dp, width), out_shape=(...  62.4 us
    pallas_call x1, Pallas kernels, shards(): pl.pallas_call(functools.partial(write_out, len(outs)), out_shape=tuple((...  2.7 us

commit v1 on v0

--- a/solution.py
+++ b/solution.py
@@ -88,6 +88,7 @@
     dc_acc,
     db_acc,
     dcum,
+    sums,
     gain_own,
     gain_in,
     red_seq,
@@ -160,6 +161,11 @@
     def as_row(col):
         return jnp.sum(jnp.where(diag, jnp.broadcast_to(col, (heads, heads)), 0.0), 0, keepdims=True)
 
+    spread_row = lax.broadcasted_iota(jnp.int32, spread.shape, 0) & (heads - 1)
+    spread_col = lax.shift_right_logical(
+        lax.broadcasted_iota(jnp.int32, spread.shape, 1), size.bit_length() - 1
+    )
+    spread[...] = jnp.where(spread_row == spread_col, 1.0, 0.0).astype(BF16)
     for move in moves[:3]:
         move.wait()
     rate = jnp.exp(column(alog_ref[...]))
@@ -186,9 +192,6 @@
 
     e_pack = pack(e_t, heads)
     to_pack = pack(jnp.exp(cum_t[span - 1 :, :] - cum_t), heads)
-    spread_row = lax.rem(lax.broadcasted_iota(jnp.int32, spread.shape, 0), heads)
-    spread_col = lax.broadcasted_iota(jnp.int32, spread.shape, 1) // size
-    spread[...] = jnp.where(spread_row == spread_col, 1.0, 0.0).astype(BF16)
     for move in moves[3:]:
         move.wait()
     bt[...] = jnp.transpose(b_ref[...].astype(F32)).astype(BF16)
@@ -198,9 +201,6 @@
 
     def part(c):
         return pl.ds(pl.multiple_of(c * width, width), width)
-
-    cb_ref[...] = dot(c_ref[...], b_ref[...], 1, 1)
-    dcb[...] = jnp.zeros_like(dcb)
 
     def role(d):
         lead = odd == d
@@ -299,6 +299,7 @@
         dv[:, cols] = dv_c
         local[0, c] = dot(bt[...], sc)
         local[1, c] = dot(ct[...], dv_c)
+        rows[:, cols] = jnp.zeros((8, width), F32)
         rows[0:1, cols] = e_c[span - 1 :, :]
         rows[2:3, cols] = dot(skip_pack[0:16], spread_c)[0:1]
         rows[4:5, cols] = jnp.sum(x_c * g_c, 0, keepdims=True)
@@ -314,6 +315,10 @@
         return carry
 
     lax.fori_loop(0, chunks, prepare, 0)
+    cb_ref[...] = dot(c_ref[...], b_ref[...], 1, 1)
+    dcb[...] = jnp.zeros_like(dcb)
+    sums[...] = jnp.zeros_like(sums)
+    dcum[...] = jnp.zeros_like(dcum)
     gain_copy.wait()
     gain_pack = pack(gain_in[...], heads)
     rows[1:2, :] = dot(gain_pack, spread[...])[15:16, :]
@@ -330,7 +335,7 @@
         for i in range(2):
             h = 2 * j + i
             pick_row = lax.broadcasted_iota(jnp.int32, (LANES, span), 0)
-            pick = jnp.where(lax.rem(pick_row, heads) == h, 1.0, 0.0).astype(BF16)
+            pick = jnp.where((pick_row & (heads - 1)) == h, 1.0, 0.0).astype(BF16)
             at_t = dot(cum_pack[...], pick)
             decay = jnp.exp(jnp.where(lower, at_t - cum_rows[pl.ds(h, 1), :], -1e30))
             weights = (cb_ref[...] * decay).astype(BF16)
@@ -357,7 +362,6 @@
     dcb_low = dcb[...]
     dc_acc[...] = dot(dcb_low.astype(BF16), b_ref[...])
     db_acc[...] = dot(jnp.transpose(dcb_low).astype(BF16), c_ref[...])
-    dcum[...] = jnp.zeros_like(dcum)
 
     def finish(i, carry):
         c = lax.rem(i + odd * half, chunks)
@@ -394,21 +398,45 @@
         rows[3:4, cols] = jnp.sum(x_c * dx_state, 0, keepdims=True) + rows[0:1, cols] * jnp.sum(
             state * adj, 0, keepdims=True
         )
+        hi, low = halves(jnp.concatenate([rows[:, cols], jnp.zeros((8, width), F32)], 0))
+        sums[...] += dot(sel, hi, 1, 1) + dot(sel, low, 1, 1)
         return carry
 
     lax.fori_loop(0, chunks, finish, 0)
 
-    gc_ref[...] = dc_acc[...].astype(BF16)
-    gb_ref[...] = db_acc[...].astype(BF16)
-    sums = jnp.concatenate([rows[3:5, :], jnp.zeros((14, feat), F32)], 0)
-    hi, low = halves(sums)
-    sel = spread[0:heads, :]
-    per_head = dot(sel, hi, 1, 1) + dot(sel, low, 1, 1)
-    lower_f = jnp.where(t_row >= t_col, 1.0, 0.0).astype(F32)
-    dla = dot(dcum[...], lower_f, precision=lax.Precision.HIGHEST) + per_head[:, 0:1]
-    gdt_ref[...] = -rate * dla
-    alog_row = as_row(jnp.sum(dla * la, 1, keepdims=True))
-    skip_row = as_row(per_head[:, 1:2])
+    per_head = sums[...]
+    last = per_head[:, 3:4]
+    alog = jnp.sum(dcum[...] * cum_rows[0:heads, :], 1, keepdims=True)
+    alog_row = as_row(alog + last * cum_rows[0:heads, span - 1 : span])
+    red_seq[me] = jnp.zeros((8, LANES), F32)
+    red_seq[me, 0:1, 0:heads] = alog_row
+    red_seq[me, 1:2, 0:heads] = as_row(per_head[:, 4:5])
+
+    def share(axis, here, count, buf, send, recv, between):
+        def copy(target, slot, o):
+            return pltpu.make_async_remote_copy(
+                src_ref=buf.at[here],
+                dst_ref=buf.at[slot],
+                send_sem=send.at[o],
+                recv_sem=recv.at[slot],
+                device_id={axis: target},
+                device_id_type=MESH,
+            )
+
+        def go(o, carry):
+            copy(lax.rem(here + o, count), here, o).start()
+            return carry
+
+        def come(o, carry):
+            source = lax.rem(here + o, count)
+            copy(source, source, o).wait_recv()
+            copy(source, here, o).wait_send()
+            return carry
+
+        lax.fori_loop(1, count, go, 0)
+        between()
+        lax.fori_loop(1, count, come, 0)
+        return jnp.sum(buf[...], 0)
 
     stores = [
         pltpu.make_async_copy(src, dst, store_sem.at[i])
@@ -422,39 +450,21 @@
             ]
         )
     ]
-    for move in stores:
-        move.start()
-    red_seq[me] = jnp.zeros((8, LANES), F32)
-    red_seq[me, 0:1, 0:heads] = alog_row
-    red_seq[me, 1:2, 0:heads] = skip_row
-
-    def share(axis, here, count, buf, send, recv):
-        def copy(target, slot, o):
-            return pltpu.make_async_remote_copy(
-                src_ref=buf.at[here],
-                dst_ref=buf.at[slot],
-                send_sem=send.at[o],
-                recv_sem=recv.at[slot],
-                device_id={axis: target},
-                device_id_type=MESH,
-            )
-
-        def go(o, carry):
-            copy(lax.rem(here + o, count), here, o).start()
-            return carry
-
-        def come(o, carry):
-            source = lax.rem(here + o, count)
-            copy(source, source, o).wait_recv()
-            copy(source, here, o).wait_send()
-            return carry
-
-        lax.fori_loop(1, count, go, 0)
-        lax.fori_loop(1, count, come, 0)
-        return jnp.sum(buf[...], 0)
-
-    red_dp[mine] = share("seq", me, n_seq, red_seq, rs_send, rs_recv)
-    total = share("dp", mine, n_dp, red_dp, rd_send, rd_recv)
+
+    def meanwhile():
+        stores[0].start()
+        stores[1].start()
+        gc_ref[...] = dc_acc[...].astype(BF16)
+        gb_ref[...] = db_acc[...].astype(BF16)
+        stores[2].start()
+        stores[3].start()
+        lower_f = jnp.where(t_row >= t_col, 1.0, 0.0).astype(F32)
+        dla = dot(dcum[...], lower_f, precision=lax.Precision.HIGHEST) + last
+        gdt_ref[...] = -rate * dla
+        stores[4].start()
+
+    red_dp[mine] = share("seq", me, n_seq, red_seq, rs_send, rs_recv, meanwhile)
+    total = share("dp", mine, n_dp, red_dp, rd_send, rd_recv, lambda: None)
     ga_ref[...] = total[0:1, 0:heads]
     gs_ref[...] = total[1:2, 0:heads]
 
@@ -483,20 +493,29 @@
         move.wait()
 
 
-def write_out(count, *refs):
+def write_out(count, pieces, *refs):
     held = refs[2 * count : 3 * count]
     load, store = refs[3 * count :]
-    loads = [pltpu.make_async_copy(refs[i], held[i], load.at[i]) for i in range(count)]
-    stores = [
-        pltpu.make_async_copy(held[i], refs[count + i], store.at[i]) for i in range(count)
-    ]
-    for copy in loads:
-        copy.start()
-    for first, second in zip(loads, stores):
+    moves = []
+    for i in range(count):
+        cuts = pieces if i < 2 else 1
+        size = held[i].shape[0] // cuts
+        for k in range(cuts):
+            at = pl.ds(k * size, size)
+            n = len(moves)
+            moves.append(
+                (
+                    pltpu.make_async_copy(refs[i].at[at], held[i].at[at], load.at[n]),
+                    pltpu.make_async_copy(held[i].at[at], refs[count + i].at[at], store.at[n]),
+                )
+            )
+    for first, _ in moves:
+        first.start()
+    for first, second in moves:
         first.wait()
         second.start()
-    for copy in stores:
-        copy.wait()
+    for _, second in moves:
+        second.wait()
 
 
 def shards(n_seq, n_dp, x_in, b_in, c_in, dt, a_log, skip, cotangent):
@@ -560,6 +579,7 @@
             pltpu.VMEM((span, state_dim), F32),
             pltpu.VMEM((span, state_dim), F32),
             pltpu.VMEM((heads, span), F32),
+            pltpu.VMEM((heads, 16), F32),
             pltpu.VMEM((16, LANES), F32),
             pltpu.VMEM((16, LANES), F32),
             pltpu.VMEM((n_seq, 8, LANES), F32),
@@ -583,12 +603,12 @@
         ),
     )(x_in[0], b_in[0], c_in[0], dt[0], a_log[None], skip[None], cotangent[0])
     y, gx, gb, gc, gdt, ga, gs = pl.pallas_call(
-        functools.partial(write_out, len(outs)),
+        functools.partial(write_out, len(outs), 4),
         out_shape=tuple(jax.ShapeDtypeStruct(o.shape, o.dtype) for o in outs),
         in_specs=[hbm] * len(outs),
         out_specs=(hbm,) * len(outs),
         scratch_shapes=[pltpu.VMEM(o.shape, o.dtype) for o in outs]
-        + [dma((len(outs),)), dma((len(outs),))],
+        + [dma((len(outs) + 6,)), dma((len(outs) + 6,))],
         compiler_params=pltpu.CompilerParams(vmem_limit_bytes=VMEM_BYTES),
     )(*outs)
     return (y[None], gx[None], gb[None], gc[None], gdt[None], ga[0], gs[0])

time: 65.9 us -> 65.6 us (level)
  no operation moved by 1% of the time
where the time goes in v1:
time: 65.6 us; the launch traced here: 65.4 us
  Pallas kernels  64.8 us (99%)
    pallas_call x1, Pallas kernels, shards(): pl.pallas_call(functools.partial(kernel, n_seq, n_dp, width), out_shape=(...  62.2 us
    pallas_call x1, Pallas kernels, shards(): pl.pallas_call(functools.partial(write_out, len(outs), 4), out_shape=tupl...  2.53 us

profile of v1, /device:TPU:0, one launch (start us, length us, event | category | flops | bytes accessed | tf_op | source)
XLA Modules:
  0.0 65.4 jit_solution(9534066113029330058)
XLA Ops:
  0.6 62.2 %shard_map.126 = (bf16[256,2048]{1,0:T(8,128)(2,1)}, bf16[256,2048]{1,0:T(8,128)(2,1)}, bf16[256,128]{1,0:T(8,128)(2,1)}, bf16[256,128]{1,0:T(8,128)(2,1)}, f32[...) custom-call(bf16[256,2048]{1,0:T(8,128)(2,1)} %bitcast.14, bf16[256,128]{1,0:T(8,128)(2,1)} %bitcast.16, ...), custom_call_target="tpu_custom_call" | custom-call | tf_op jit(solution)/shard_map/pallas_call | solution.py:533
  62.9 2.5 %shard_map.127 = (bf16[256,2048]{1,0:T(8,128)(2,1)}, bf16[256,2048]{1,0:T(8,128)(2,1)}, bf16[256,128]{1,0:T(8,128)(2,1)}, bf16[256,128]{1,0:T(8,128)(2,1)}, f32[...) custom-call(bf16[256,2048]{1,0:T(8,128)(2,1)} %get-tuple-element.21.refs_0_, ...), custom_call_target="tpu_custom_call" | custom-call | tf_op jit(solution)/shard_map/pallas_call | solution.py:605

commit v2 on v1

--- a/solution.py
+++ b/solution.py
@@ -324,30 +324,45 @@
     rows[1:2, :] = dot(gain_pack, spread[...])[15:16, :]
 
 
-    def inner(j, carry):
+    mid = span // 2
+    low_part, high_part = slice(0, mid), slice(mid, span)
+    lane = lax.broadcasted_iota(jnp.int32, (span, 2 * size), 1)
+    lower = lax.broadcasted_iota(jnp.int32, (mid, mid), 0) >= lax.broadcasted_iota(
+        jnp.int32, (mid, mid), 1
+    )
+    pick_row = lax.broadcasted_iota(jnp.int32, (LANES, mid), 0) & (heads - 1)
+
+    def inner(j):
         cols = pl.ds(pl.multiple_of(j * 2 * size, 2 * size), 2 * size)
         x2 = x_ref[:, cols]
         g2 = g_ref[:, cols]
-        lane = lax.broadcasted_iota(jnp.int32, (span, 2 * size), 1)
-        lower = t_row >= t_col
         y2, dx2 = [], []
-        total = dcb[...]
+        t00, t1 = 0.0, 0.0
         for i in range(2):
             h = 2 * j + i
-            pick_row = lax.broadcasted_iota(jnp.int32, (LANES, span), 0)
-            pick = jnp.where((pick_row & (heads - 1)) == h, 1.0, 0.0).astype(BF16)
+            pick = jnp.where(pick_row == h, 1.0, 0.0).astype(BF16)
             at_t = dot(cum_pack[...], pick)
-            decay = jnp.exp(jnp.where(lower, at_t - cum_rows[pl.ds(h, 1), :], -1e30))
-            weights = (cb_ref[...] * decay).astype(BF16)
-            y2.append(dot(weights, x2))
-            dx2.append(dot(weights, g2, 0, 0))
+            row = cum_rows[pl.ds(h, 1), :]
+            at_low, at_high = at_t[low_part], at_t[high_part]
+            d00 = jnp.exp(jnp.where(lower, at_low - row[:, low_part], -1e30))
+            d10 = jnp.exp(at_high - row[:, low_part])
+            d11 = jnp.exp(jnp.where(lower, at_high - row[:, high_part], -1e30))
+            d1 = jnp.concatenate([d10, d11], 1)
+            w00 = (cb_ref[low_part, low_part] * d00).astype(BF16)
+            w1 = (cb_ref[high_part, :] * d1).astype(BF16)
+            y2.append(jnp.concatenate([dot(w00, x2[low_part]), dot(w1, x2)], 0))
+            left = jnp.concatenate([w00, w1[:, low_part]], 0)
+            dx2.append(
+                jnp.concatenate([dot(left, g2, 0, 0), dot(w1[:, high_part], g2[high_part], 0, 0)], 0)
+            )
             own_lanes = (lane < size) if i == 0 else (lane >= size)
             g_own = jnp.where(own_lanes, g2.astype(F32), 0.0).astype(BF16)
-            total = total + dot(g_own, x2, 1, 1) * decay
-        dcb[...] = total
+            t00 = t00 + dot(g_own[low_part], x2[low_part], 1, 1) * d00
+            t1 = t1 + dot(g_own[high_part], x2, 1, 1) * d1
+        dcb[low_part, low_part] += t00
+        dcb[high_part, :] += t1
         y_acc[:, cols] = jnp.where(lane < size, y2[0], y2[1])
         dx_acc[:, cols] = jnp.where(lane < size, dx2[0], dx2[1])
-        return carry
 
     per_chunk = width // (2 * size)
     upper_half = jnp.where(place >= pairs // 2, 1, 0)
@@ -355,7 +370,9 @@
     def middle(i, carry):
         late = i // half
         step(upper_half + late - 2 * late * upper_half, lax.rem(i, half) + odd * half)
-        return lax.fori_loop(i * per_chunk, (i + 1) * per_chunk, inner, carry)
+        for k in range(per_chunk):
+            inner(i * per_chunk + k)
+        return carry
 
     lax.fori_loop(0, chunks, middle, 0)
 

time: 65.6 us -> 64.9 us (0.989)
  Pallas kernels: 64.8 us -> 64.1 us
where the time goes in v2:
time: 64.9 us; the launch traced here: 64.8 us
  Pallas kernels  64.1 us (99%)
    pallas_call x1, Pallas kernels, shards(): pl.pallas_call(functools.partial(kernel, n_seq, n_dp, width), out_shape=(...  61.6 us
    pallas_call x1, Pallas kernels, shards(): pl.pallas_call(functools.partial(write_out, len(outs), 4), out_shape=tupl...  2.53 us

profile of v2, /device:TPU:0, one launch (start us, length us, event | category | flops | bytes accessed | tf_op | source)
XLA Modules:
  0.0 64.8 jit_solution(4653002186091013248)
XLA Ops:
  0.6 61.6 %shard_map.126 = (bf16[256,2048]{1,0:T(8,128)(2,1)}, bf16[256,2048]{1,0:T(8,128)(2,1)}, bf16[256,128]{1,0:T(8,128)(2,1)}, bf16[256,128]{1,0:T(8,128)(2,1)}, f32[...) custom-call(bf16[256,2048]{1,0:T(8,128)(2,1)} %bitcast.14, bf16[256,128]{1,0:T(8,128)(2,1)} %bitcast.16, ...), custom_call_target="tpu_custom_call" | custom-call | tf_op jit(solution)/shard_map/pallas_call | solution.py:550
  62.2 2.5 %shard_map.127 = (bf16[256,2048]{1,0:T(8,128)(2,1)}, bf16[256,2048]{1,0:T(8,128)(2,1)}, bf16[256,128]{1,0:T(8,128)(2,1)}, bf16[256,128]{1,0:T(8,128)(2,1)}, f32[...) custom-call(bf16[256,2048]{1,0:T(8,128)(2,1)} %get-tuple-element.21.refs_0_, ...), custom_call_target="tpu_custom_call" | custom-call | tf_op jit(solution)/shard_map/pallas_call | solution.py:622
